TPU v7x, 512 devices: a whole 4x4x16 slice. The times are simulated.
512 devices in a mesh: row: 32 (over y, z_lo), col: 16 (over z_hi, x, core).
Axes of the slice: x: 4, y: 4, z: 16 (z_hi: 2, z_lo: 8; z = z_hi * 8 + z_lo), core: 2. Of those that a mesh axis runs over, the one named last changes fastest.
Arguments:
- blocks: bfloat16 [32, 16, 40, 128, 128], P('row', 'col'), may hold values from -2.5 to 2.5
- block_rows: int32 [32, 16, 40], P('row', 'col'), may hold values from -1 to 12, as said below
- block_cols: int32 [32, 16, 40], P('row', 'col'), may hold values from -1 to 25, as said below
Outputs:
- product: bfloat16 [32, 16, 40, 128, 128], P('row', 'col')
Inputs may be any that keep to these rules, and one draw needn't show every extreme that they name: On each device the live slots name distinct (row, column) pairs; an empty slot has -1 in block_rows and block_cols alike, and slots are in no particular order. Each half of a device's block columns (the first 13 or the last 13) holds at least 10 and at most 20 stored blocks, and some half in the matrix holds exactly 20. `block_cols`: see block_rows: the same slots are live.
All inputs are finite; a program needn't handle non-finite values.
Results may differ from a plain program's by a relative error of at most 0.001.
Values may be sent and summed in bfloat16 or wider, within the bound.
A program may use at most 64 MiB of HBM per device.

v0:
```python
import jax
import jax.numpy as jnp
from jax import lax
from jax.sharding import PartitionSpec as P

BROW = 13


def broadcast(value, axis, root):
    mine = lax.axis_index(axis) == root
    return lax.psum(jnp.where(mine, value, jnp.zeros_like(value)), axis)


def shortened(value):
    return jax.tree.map(lambda a: a.astype(jnp.bfloat16) if a.dtype == jnp.float32 else a, value)


def from_behind(value, axis, steps):
    count = lax.axis_size(axis)
    pairs = [(source, (source + steps) % count) for source in range(count)]
    return lax.ppermute(value, axis, pairs)


def make_table(position_rows, slot_cols, height, tile_width):
    places_total = position_rows.shape[0]
    cell_ids = jnp.arange(height * tile_width, dtype=jnp.int32)
    cell_code = jnp.where(position_rows >= 0, position_rows * tile_width + slot_cols, -1)
    pairing_hits = cell_code[:, None] == cell_ids[None, :]
    position_index = jnp.arange(places_total, dtype=jnp.int32)[:, None]
    located_position = jnp.sum(jnp.where(pairing_hits, position_index, 0), axis=0)
    lookup_register = jnp.where(jnp.any(pairing_hits, axis=0), located_position, places_total)
    return lookup_register.reshape(height, tile_width)


def pick_columns(lookup_register, wanted):
    onehot = wanted[:, None] == jnp.arange(lookup_register.shape[1], dtype=jnp.int32)[None, :]
    return jnp.sum(jnp.where(onehot[:, None, :], lookup_register[None, :, :], 0), axis=2)


def panel_product(left_part, right_part, resident_rows, own_cols):
    left_blocks, left_rows, left_cols = left_part
    right_blocks, target_lines, right_cols = right_part
    tile_side_size = right_blocks.shape[1]
    places_total = resident_rows.shape[0]
    left_table = make_table(left_rows, left_cols, BROW, BROW)
    right_table = make_table(target_lines, right_cols, BROW, 2 * BROW)
    left_index = pick_columns(left_table, jnp.maximum(resident_rows, 0))
    right_index = pick_columns(right_table, jnp.maximum(own_cols, 0))
    zero_block = jnp.zeros((1, tile_side_size, tile_side_size), right_blocks.dtype)
    left_padded = jnp.concatenate([left_blocks, zero_block], axis=0)
    right_padded = jnp.concatenate([right_blocks, zero_block], axis=0)

    def group_product(indices):
        source_cluster = left_padded[indices[0]]
        right_group = right_padded[indices[1]]
        return jnp.einsum(
            "gkxi,gkxj->gij", source_cluster, right_group, preferred_element_type=jnp.float32
        )

    block_families = places_total // 8
    interim_summands = lax.map(
        group_product,
        (left_index.reshape(block_families, 8, BROW), right_index.reshape(block_families, 8, BROW)),
    )
    return interim_summands.reshape(places_total, tile_side_size, tile_side_size)


def source_tiles_data(tile_blocks, position_rows, slot_cols, vertical_share):
    inside = (
        (position_rows >= 0)
        & (slot_cols >= vertical_share * BROW)
        & (slot_cols < vertical_share * BROW + BROW)
    )
    local_rows = jnp.where(inside, position_rows, -1)
    local_cols = jnp.where(inside, slot_cols - vertical_share * BROW, -1)
    return (tile_blocks, local_rows, local_cols)


def fetch_left(payload, root_index):
    return (
        broadcast(payload[0], "col", root_index),
        broadcast(shortened(payload[1]), "col", root_index),
        broadcast(shortened(payload[2]), "col", root_index),
    )


def shards(blocks, block_rows, block_cols):
    tile_blocks = blocks[0, 0]
    position_rows = block_rows[0, 0]
    slot_cols = block_cols[0, 0]
    row_position = lax.axis_index("row")
    vertical_share = row_position % 2
    root_index = row_position // 2
    first_payload = source_tiles_data(tile_blocks, position_rows, slot_cols, vertical_share)
    later_blocks, later_rows, later_cols = from_behind(
        (tile_blocks, position_rows, slot_cols), "row", -1
    )
    second_payload = source_tiles_data(later_blocks, later_rows, later_cols, vertical_share)
    first_left = fetch_left(first_payload, root_index)
    second_left = fetch_left(second_payload, root_index)
    summed = panel_product(
        first_left, (tile_blocks, position_rows, slot_cols), position_rows, slot_cols
    )
    summed = summed + panel_product(
        second_left, (later_blocks, later_rows, later_cols), position_rows, slot_cols
    )
    result = jnp.where((position_rows >= 0)[:, None, None], summed, jnp.float32(0.0)).astype(
        jnp.bfloat16
    )
    return result[None, None]


def solution(mesh):
    return jax.shard_map(
        shards,
        mesh=mesh,
        in_specs=(P("row", "col", None, None, None), P("row", "col", None), P("row", "col", None)),
        out_specs=P("row", "col", None, None, None),
        check_vma=False,
    )
```

profile of v0, /device:TPU:24, one launch (start us, length us, event | category | flops | bytes accessed | tf_op | source)
XLA Modules:
  0.0 474.6 jit_solution(8692382213202309966)
XLA Ops:
  6.5 13.3 %collective-permute-start.2 = (bf16[40,128,128]{2,1,0:T(8,128)(2,1)}, bf16[40,128,128]{2,1,0:T(8,128)(2,1)S(1)}, u32[]{:S(2)}, u32[]{:S(2)}) collective-permute-start(bf16[40,128,128]{2,1,0:T(8,128)(2,1)} %bitcast.93), channel_id=1, source_target_pairs={{0,496},{16,0},{32,16},{48,32},{64,48},{80,64},{96,80},{112,96},{1... | collective-permute-start | bytes 3932168 | tf_op jit(solution)/shard_map/ppermute | solution.py:21
  19.9 2.0 collective-permute-start
  21.9 2.0 collective-permute-start.1
  25.3 2.5 broadcast_select_fusion.1
  27.8 20.4 %collective-permute-done.2 = bf16[40,128,128]{2,1,0:T(8,128)(2,1)S(1)} collective-permute-done((bf16[40,128,128]{2,1,0:T(8,128)(2,1)}, bf16[40,128,128]{2,1,0:T(8,128)(2,1)S(1)}, u32[]{:S(2)}, u32[]{:S(2)}) %collective-permute-start.2) | collective-permute-done | bytes 1310752 | tf_op jit(solution)/shard_map/ppermute | solution.py:21
  48.2 1.2 broadcast_select_fusion
  49.7 1.2 concatenate.13
  50.9 17.2 %all-reduce.4 = (s32[40]{0:T(128)S(1)}, s32[40]{0:T(128)S(1)}, s32[40]{0:T(128)S(1)}, s32[40]{0:T(128)S(1)}) all-reduce(s32[40]{0:T(128)S(1)} %get-tuple-element.125, s32[40]{0:T(128)S(1)} %get-tuple-element.126, s32[40]{0:T(128)S(1)} %get-tuple-element.122, s32[40]{0:T(128)S(1)} %get-tuple-element.123), channel_id=1, replica_groups=mesh['row'=32,'col'=16] {'col'}, use_global_device_ids=true, to_apply=%region_11.12 | all-reduce | flops 160 | bytes 1280 | tf_op jit(solution)/shard_map/psum | solution.py:11
  69.6 1.2 concatenate.15
  70.9 275.0 %all-reduce.8.cloned.1.call-done = (bf16[40,128,128]{2,1,0:T(8,128)(2,1)}, bf16[40,128,128]{2,1,0:T(8,128)(2,1)}) async-done(((bf16[40,128,128]{2,1,0:T(8,128)(2,1)}, bf16[40,128,128]{2,1,0:T(8,128)(2,1)}), (bf16[40,128,128]{2,1,0:T(8,128)(2,1)}, bf16[40,128,128]{2,1,0:T(8,128)(2,1)})) %all-reduce.8.cloned.1.call-update) | async-done | bytes 2621456 | tf_op jit(solution)/shard_map/psum | solution.py:11
  345.9 2.5 concatenate.14
  348.4 1.8 broadcast.178.clone.1
  350.2 54.4 %while.21 = (s32[]{:T(128)}, f32[5,8,128,128]{3,2,1,0:T(8,128)}, s32[5,8,13]{2,1,0:T(8,128)S(1)}, bf16[41,128,128]{2,1,0:T(8,128)(2,1)}, s32[5,8,13]{2,1,0:T(8,1...) while((s32[]{:T(128)}, f32[5,8,128,128]{3,2,1,0:T(8,128)}, s32[5,8,13]{2,1,0:T(8,128)S(1)}, ...), condition=%wide.region_21.22_spmd, body=%wide.region_20.21_spmd.sunk | while | flops 436210304 | bytes 20985296 | solution.py:61
  350.3 2.5 gather_fusion.2
  353.0 4.2 gather_fusion.3
  357.2 3.9 fusion.21
  361.2 2.5 gather_fusion.2
  363.8 4.2 gather_fusion.3
  368.0 3.9 fusion.21
  372.1 2.5 gather_fusion.2
  374.7 4.2 gather_fusion.3
  378.9 3.9 fusion.21
  383.0 2.5 gather_fusion.2
  385.6 4.2 gather_fusion.3
  389.8 3.9 fusion.21
  393.8 2.5 gather_fusion.2
  396.5 4.2 gather_fusion.3
  400.7 3.9 fusion.21
  404.6 2.5 concatenate.12
  407.1 1.8 broadcast.178.clone
  409.0 54.4 %while.20 = (s32[]{:T(128)}, f32[5,8,128,128]{3,2,1,0:T(8,128)}, s32[5,8,13]{2,1,0:T(8,128)S(1)}, bf16[41,128,128]{2,1,0:T(8,128)(2,1)}, s32[5,8,13]{2,1,0:T(8,1...) while((s32[]{:T(128)}, f32[5,8,128,128]{3,2,1,0:T(8,128)}, s32[5,8,13]{2,1,0:T(8,128)S(1)}, ...), condition=%wide.region_10.11_spmd, body=%wide.region_9.10_spmd.sunk | while | flops 436210304 | bytes 20985296 | solution.py:61
  409.1 2.5 gather_fusion
  411.7 4.2 gather_fusion.1
  415.9 3.9 fusion.18
  419.9 2.5 gather_fusion
  422.6 4.2 gather_fusion.1
  426.8 3.9 fusion.18
  430.8 2.5 gather_fusion
  433.4 4.2 gather_fusion.1
  437.7 3.9 fusion.18
  441.7 2.5 gather_fusion
  444.3 4.2 gather_fusion.1
  448.5 4.0 fusion.18
  452.6 2.5 gather_fusion
  455.2 4.2 gather_fusion.1
  459.4 3.9 fusion.18
  463.4 3.0 add.110
  466.4 1.4 select_convert_fusion
  (84 shorter events, 5.0 us)
Async XLA Ops:
  6.5 339.3 %all-reduce.8.cloned.1.call-start = ((), (), s32[]{:S(2)}) async-start(), calls=%async_computation | async-start | bytes 5242880 | tf_op jit(solution)/shard_map/psum | solution.py:11
  6.5 41.7 %collective-permute-start.2 = (bf16[40,128,128]{2,1,0:T(8,128)(2,1)}, bf16[40,128,128]{2,1,0:T(8,128)(2,1)S(1)}, u32[]{:S(2)}, u32[]{:S(2)}) collective-permute-start(bf16[40,128,128]{2,1,0:T(8,128)(2,1)} %bitcast.93), channel_id=1, source_target_pairs={{0,496},{16,0},{32,16},{48,32},{64,48},{80,64},{96,80},{112,96},{1... | collective-permute-start | bytes 3932168 | tf_op jit(solution)/shard_map/ppermute | solution.py:21
  19.9 31.0 %collective-permute-start = (s32[40]{0:T(128)}, s32[40]{0:T(128)S(1)}, u32[]{:S(2)}, u32[]{:S(2)}) collective-permute-start(s32[40]{0:T(128)} %bitcast.100), channel_id=1, source_target_pairs={{0,496},{16,0},{32,16},{48,32},{64,48},{80,64},{96,80},{112,96},{1... | collective-permute-start | bytes 488 | tf_op jit(solution)/shard_map/ppermute | solution.py:21
  21.9 29.0 %collective-permute-start.1 = (s32[40]{0:T(128)}, s32[40]{0:T(128)S(1)}, u32[]{:S(2)}, u32[]{:S(2)}) collective-permute-start(s32[40]{0:T(128)} %bitcast.101), channel_id=1, source_target_pairs={{0,496},{16,0},{32,16},{48,32},{64,48},{80,64},{96,80},{112,96},{1... | collective-permute-start | bytes 488 | tf_op jit(solution)/shard_map/ppermute | solution.py:21
  27.8 22.0 %copy-start = (bf16[1,1,40,128,128]{4,3,2,1,0:T(8,128)(2,1)S(1)}, bf16[1,1,40,128,128]{4,3,2,1,0:T(8,128)(2,1)}, u32[]{:S(2)}) copy-start(bf16[1,1,40,128,128]{4,3,2,1,0:T(8,128)(2,1)} %param.7) | copy-start | bytes 3932164
Sparse Core Ops, SparseCore 0:
  49.5 296.2 all-reduce.7
where the time goes:
time: 476 us; the launch traced here: 475 us
  waiting for transfers between devices  295 us (62%)
  local copies, waits for them, and re-layouts  81 us (17%)
  matrix products  39.3 us (8%)
  starting transfers between devices  17.4 us (4%)
  blocking collectives  17.2 us (4%)
  between operations  13.5 us (3%)
  other arithmetic  10.7 us (2%)
    psum x1, waiting for transfers between devices, broadcast(): return lax.psum(jnp.where(mine, value, jnp.zeros_like(value)), axis)  275 us
    gather x10, local copies, waits for them, and re-layouts, group_product(): right_group = right_padded[indices[1]]  42.2 us
    dot_general x10, matrix products, group_product(): jnp.einsum('gkxi,gkxj->gij', source_cluster, right_group, preferred_eleme...  39.3 us
    gather x10, local copies, waits for them, and re-layouts, group_product(): source_cluster = left_padded[indices[0]]  25.3 us
    ppermute x3, waiting for transfers between devices, from_behind(): return lax.ppermute(value, axis, pairs)  20.5 us
    ppermute x3, starting transfers between devices, from_behind(): return lax.ppermute(value, axis, pairs)  17.4 us
    psum x1, blocking collectives, broadcast(): return lax.psum(jnp.where(mine, value, jnp.zeros_like(value)), axis)  17.2 us
  transfers between devices with their start and end apart: 4, of which 2 were waited for; matrix products, arithmetic and copies ran while one was open for 2% of the time, Pallas kernels for 0%

commit v1 on v0

v1 whole, which is shorter than its diff:
```python
import functools

import jax
import jax.numpy as jnp
from jax import lax
from jax.experimental import pallas as pl
from jax.experimental.pallas import tpu as pltpu
from jax.sharding import PartitionSpec as P

MESH = pl.DeviceIdType.MESH
BS = 128
BROW = 13
HALF = 20
SLOTS = 40
N_ROW = 32
N_COL = 16
PIECES = 4
PER = HALF // PIECES
PIECE_ROWS = PER * BS + 16
SHIFT_PARTS = 5
SHIFT_SLOTS = SLOTS // SHIFT_PARTS


def gather_kernel(
    rows_s, cols_s, blocks,
    left, shifted, shifted_meta,
    held, stage, meta, order_v, order_s,
    local_sem, root_sem, piece_sem, z_sem, x_sem, core_sem,
    shift_send, shift_recv, meta_send, meta_recv,
):
    r, c = lax.axis_index("row"), lax.axis_index("col")
    zh, x, k = c // 8, (c // 2) % 4, c % 2
    above, below = (r + 1) % N_ROW, (r + N_ROW - 1) % N_ROW
    root_col = r // 2
    primary = zh == root_col // 8
    first_root = c == root_col
    second_root = c == below // 2
    own_first = jnp.logical_and(first_root, k == 0)

    def at(x_of, k_of, zh_of=zh):
        return zh_of * 8 + x_of * 2 + k_of

    ring = [(x + d) % 4 for d in (1, 3, 2)]
    barrier = pltpu.get_barrier_semaphore()

    def greet(row, col):
        pl.semaphore_signal(barrier, inc=1, device_id=(row, col), device_id_type=MESH)

    greet(above, c)
    greet(r, at(x, 1 - k))
    for x_of in ring:
        greet(r, at(x_of, k))

    @pl.when(jnp.logical_not(primary))
    def _():
        greet(r, at(x, k, 1 - zh))

    @pl.when(jnp.logical_and(primary, jnp.logical_and(k == 0, jnp.logical_not(first_root))))
    def _():
        greet(r, root_col)

    @pl.when(jnp.logical_and(primary, k == 1))
    def _():
        greet(above, root_col)

    is_root = jnp.logical_or(first_root, second_root)

    @pl.when(is_root)
    def _():
        pltpu.make_async_copy(blocks, held, local_sem.at[0]).start()

    lane = lax.broadcasted_iota(jnp.int32, (8, 128), 1)
    sub = lax.broadcasted_iota(jnp.int32, (8, 128), 0)

    def place(t, carry):
        n0, n1, own, order, line, column = carry
        a, b = rows_s[t], cols_s[t]
        half = jnp.where(b >= BROW, 1, 0)
        live = jnp.where(a >= 0, 1, 0)
        spot = jnp.where(a >= 0, jnp.where(b >= BROW, n1, n0), 127)
        mine = jnp.logical_and(lane == spot, sub == half)
        own = jnp.where(lane == t, jnp.where(sub == 0, a, b), own)
        order = jnp.where(mine, t, order)
        line = jnp.where(mine, a, line)
        column = jnp.where(mine, b - BROW * half, column)
        return n0 + live * (1 - half), n1 + live * half, own, order, line, column

    zero = jnp.zeros((8, 128), jnp.int32)
    _, _, own, order, line, column = lax.fori_loop(
        0, SLOTS, place, (jnp.int32(0), jnp.int32(0), zero, zero, zero - 1, zero)
    )
    meta[...] = own

    @pl.when(is_root)
    def _():
        order_v[...] = order
        to_scalars = pltpu.make_async_copy(order_v, order_s, local_sem.at[1])
        to_scalars.start()
        pltpu.make_async_copy(blocks, held, local_sem.at[0]).wait()
        to_scalars.wait()

    sub16 = lax.broadcasted_iota(jnp.int32, (16, 128), 0)

    def pack(role, half):
        rows_of = jnp.where(half == 0, line[0:1, :], line[1:2, :])
        cols_of = jnp.where(half == 0, column[0:1, :], column[1:2, :])
        tile = jnp.where(sub16 == 0, rows_of, jnp.where(sub16 == 1, cols_of, 0))
        tile = tile.astype(jnp.float32).astype(jnp.bfloat16)
        for i in range(PIECES):
            for j in range(PER):
                stage[role, i, j * BS:(j + 1) * BS, :] = held[order_s[half, i * PER + j]]
            stage[role, i, PER * BS:, :] = tile

    @pl.when(first_root)
    def _():
        pack(0, r % 2)

    @pl.when(second_root)
    def _():
        pack(1, below % 2)

    def remote(src, dst, send, recv, row, col):
        return pltpu.make_async_remote_copy(
            src_ref=src, dst_ref=dst, send_sem=send, recv_sem=recv, device_id=(row, col), device_id_type=MESH
        )

    def root_copy(role, i, row):
        return remote(
            stage.at[role, i], left.at[role, i], root_sem.at[role, i], piece_sem.at[role, i], row, at(i, role)
        )

    def keep_own():
        return pltpu.make_async_copy(stage.at[0, x], left.at[0, x], local_sem.at[2])

    def shift_copy(i):
        part = pl.ds(i * SHIFT_SLOTS, SHIFT_SLOTS)
        return remote(blocks.at[part], shifted.at[part], shift_send.at[i], shift_recv.at[i], below, c)

    def z_copy():
        return remote(left.at[k, x], left.at[k, x], z_sem.at[0], piece_sem.at[k, x], r, at(x, k, 1 - zh))

    def x_copy(n):
        return remote(left.at[k, x], left.at[k, x], x_sem.at[n], piece_sem.at[k, x], r, at(ring[n], k))

    def core_copy(n, i):
        return remote(left.at[k, i], left.at[k, i], core_sem.at[n], piece_sem.at[k, i], r, at(x, 1 - k))

    def arrived(panel, i):
        remote(left.at[panel, i], left.at[panel, i], core_sem.at[0], piece_sem.at[panel, i], r, at(x, 1 - k)).wait_recv()

    meta_copy = remote(meta, shifted_meta, meta_send.at[0], meta_recv.at[0], below, c)

    sends = (
        5
        + jnp.where(primary, 1, 0)
        + jnp.where(first_root, 4 - jnp.where(k == 0, 1, 0), 0)
        + jnp.where(second_root, 4, 0)
    )
    pl.semaphore_wait(barrier, sends)

    @pl.when(first_root)
    def _():
        for i in range(PIECES):
            @pl.when(jnp.logical_not(jnp.logical_and(own_first, x == i)))
            def _():
                root_copy(0, i, r).start()

    @pl.when(second_root)
    def _():
        for i in range(PIECES):
            root_copy(1, i, below).start()

    @pl.when(own_first)
    def _():
        keep_own().start()

    meta_copy.start()
    for i in range(SHIFT_PARTS):
        shift_copy(i).start()

    @pl.when(own_first)
    def _():
        keep_own().wait()

    @pl.when(jnp.logical_not(own_first))
    def _():
        arrived(k, x)

    @pl.when(primary)
    def _():
        z_copy().start()

    for n in range(3):
        x_copy(n).start()
    core_copy(0, x).start()
    for n in range(3):
        arrived(k, ring[n])
        core_copy(1 + n, ring[n]).start()
    for i in range(PIECES):
        arrived(1 - k, i)

    @pl.when(first_root)
    def _():
        for i in range(PIECES):
            @pl.when(jnp.logical_not(jnp.logical_and(own_first, x == i)))
            def _():
                root_copy(0, i, r).wait_send()

    @pl.when(second_root)
    def _():
        for i in range(PIECES):
            root_copy(1, i, below).wait_send()

    @pl.when(primary)
    def _():
        z_copy().wait_send()

    for n in range(3):
        x_copy(n).wait_send()
    core_copy(0, x).wait_send()
    for n in range(3):
        core_copy(1 + n, ring[n]).wait_send()
    meta_copy.wait()
    for i in range(SHIFT_PARTS):
        shift_copy(i).wait()


def gather(rows, cols, blocks):
    any_space = pl.BlockSpec(memory_space=pl.ANY)
    scalars = pl.BlockSpec(memory_space=pltpu.SMEM)
    dma = pltpu.SemaphoreType.DMA
    return pl.pallas_call(
        gather_kernel,
        name="gather",
        out_shape=(
            jax.ShapeDtypeStruct((2, PIECES, PIECE_ROWS, BS), jnp.bfloat16),
            jax.ShapeDtypeStruct((SLOTS, BS, BS), jnp.bfloat16),
            jax.ShapeDtypeStruct((8, 128), jnp.int32),
        ),
        in_specs=[scalars, scalars, any_space],
        out_specs=(any_space, any_space, any_space),
        scratch_shapes=[
            pltpu.VMEM((SLOTS, BS, BS), jnp.bfloat16),
            pltpu.VMEM((2, PIECES, PIECE_ROWS, BS), jnp.bfloat16),
            pltpu.VMEM((8, 128), jnp.int32),
            pltpu.VMEM((8, 128), jnp.int32),
            pltpu.SMEM((8, 128), jnp.int32),
            dma((3,)),
            dma((2, PIECES)),
            dma((2, PIECES)),
            dma((1,)),
            dma((3,)),
            dma((PIECES,)),
            dma((SHIFT_PARTS,)),
            dma((SHIFT_PARTS,)),
            dma((1,)),
            dma((1,)),
        ],
        compiler_params=pltpu.CompilerParams(
            collective_id=0, has_side_effects=True, vmem_limit_bytes=16 * 1024 * 1024
        ),
    )(rows, cols, blocks)


def multiply_kernel(
    rows_s, cols_s, shifted_s, blocks, shifted, left, out,
    coords_v, coords_s, left_mask, right_mask, left_slot, right_slot, total, sem,
):
    for p in range(2):
        coords_v[p] = left[p, 0, PER * BS:, :].astype(jnp.float32).astype(jnp.int32)
    to_scalars = pltpu.make_async_copy(coords_v, coords_s, sem)
    to_scalars.start()
    out[...] = jnp.zeros_like(out)

    @pl.loop(0, 32)
    def _(i):
        left_mask[i] = 0
        right_mask[i] = 0
        right_mask[i + 32] = 0

    def add_right(p, a, b, t):
        @pl.when(a >= 0)
        def _():
            right_mask[p * 32 + b] = right_mask[p * 32 + b] | (1 << a)
            right_slot[p * 512 + b * 16 + a] = t

    @pl.loop(0, SLOTS)
    def _(t):
        add_right(0, rows_s[t], cols_s[t], t)
        add_right(1, shifted_s[0, t], shifted_s[1, t], t)

    to_scalars.wait()

    @pl.loop(0, HALF)
    def _(j):
        for p in range(2):
            a, b = coords_s[p, 0, j], coords_s[p, 1, j]

            @pl.when(a >= 0)
            def _():
                left_mask[p * 16 + b] = left_mask[p * 16 + b] | (1 << a)
                left_slot[p * 256 + b * 16 + a] = j

    @pl.loop(0, SLOTS)
    def _(t):
        a, b = rows_s[t], cols_s[t]

        @pl.when(a >= 0)
        def _():
            meet = [left_mask[p * 16 + a] & right_mask[p * 32 + b] for p in range(2)]

            @pl.when((meet[0] | meet[1]) != 0)
            def _():
                total[...] = jnp.zeros_like(total)
                for p, right in enumerate((blocks, shifted)):
                    @pl.when(meet[p] != 0)
                    def _():
                        @pl.loop(0, BROW)
                        def _(m):
                            @pl.when(((meet[p] >> m) & 1) != 0)
                            def _():
                                j = left_slot[p * 256 + a * 16 + m]
                                piece = j // PER
                                start = pl.multiple_of((j - piece * PER) * BS, BS)
                                total[...] += lax.dot_general(
                                    left[p, piece, pl.ds(start, BS), :],
                                    right[right_slot[p * 512 + b * 16 + m]],
                                    (((0,), (0,)), ((), ())),
                                    preferred_element_type=jnp.float32,
                                )
                out[t] = total[...].astype(jnp.bfloat16)


def multiply(rows, cols, shifted_meta, blocks, shifted, left):
    scalars = pl.BlockSpec(memory_space=pltpu.SMEM)
    vectors = pl.BlockSpec(memory_space=pltpu.VMEM)
    return pl.pallas_call(
        multiply_kernel,
        name="multiply",
        out_shape=jax.ShapeDtypeStruct((SLOTS, BS, BS), jnp.bfloat16),
        in_specs=[scalars, scalars, scalars, vectors, vectors, vectors],
        out_specs=vectors,
        scratch_shapes=[
            pltpu.VMEM((2, 16, 128), jnp.int32),
            pltpu.SMEM((2, 16, 128), jnp.int32),
            pltpu.SMEM((32,), jnp.int32),
            pltpu.SMEM((64,), jnp.int32),
            pltpu.SMEM((512,), jnp.int32),
            pltpu.SMEM((1024,), jnp.int32),
            pltpu.VMEM((BS, BS), jnp.float32),
            pltpu.SemaphoreType.DMA,
        ],
        compiler_params=pltpu.CompilerParams(vmem_limit_bytes=32 * 1024 * 1024),
    )(rows, cols, shifted_meta, blocks, shifted, left)


def shards(blocks, block_rows, block_cols):
    blocks, rows, cols = blocks[0, 0], block_rows[0, 0], block_cols[0, 0]
    left, shifted, shifted_meta = gather(rows, cols, blocks)
    product = multiply(rows, cols, shifted_meta, blocks, shifted, left)
    return product[None, None]


def solution(mesh):
    return jax.shard_map(
        shards,
        mesh=mesh,
        in_specs=(P("row", "col", None, None, None), P("row", "col", None), P("row", "col", None)),
        out_specs=P("row", "col", None, None, None),
        check_vma=False,
    )
```

time: 476 us -> 88.2 us (0.19)
  the two profiles are of different devices: /device:TPU:24 before, /device:TPU:223 now
where the time goes in v1:
time: 88.2 us; the launch traced here: 88 us
  Pallas kernels  85.3 us (97%)
  local copies, waits for them, and re-layouts  2.66 us (3%)
    pallas_call x1, Pallas kernels, gather(): pl.pallas_call(gather_kernel, name='gather', out_shape=(jax.ShapeDtypeStr...  79.1 us
    pallas_call x1, Pallas kernels, multiply(): pl.pallas_call(multiply_kernel, name='multiply', out_shape=jax.ShapeDtype...  6.2 us
    unnamed x12, local copies, waits for them, and re-layouts  2.66 us

profile of v1, /device:TPU:223, one launch (start us, length us, event | category | flops | bytes accessed | tf_op | source)
XLA Modules:
  0.0 88.0 jit_solution(1453497093999932521)
XLA Ops:
  0.0 0.0 copy-start.5
  0.0 0.0 copy-start.3
  0.0 0.0 copy-start
  0.0 1.3 %copy-done = bf16[1,1,40,128,128]{4,3,2,1,0:T(8,128)(2,1)S(1)} copy-done((bf16[1,1,40,128,128]{4,3,2,1,0:T(8,128)(2,1)S(1)}, bf16[1,1,40,128,128]{4,3,2,1,0:T(8,128)(2,1)}, u32[]{:S(2)}) %copy-start) | copy-done | bytes 1310744
  1.3 0.0 copy-start.2
  1.4 0.7 copy-done.2
  2.0 0.0 copy-start.4
  2.0 0.7 copy-done.4
  2.7 0.0 copy-start.1
  2.7 79.1 %gather.1 = (bf16[2,4,656,128]{3,2,1,0:T(8,128)(2,1)S(1)}, bf16[40,128,128]{2,1,0:T(8,128)(2,1)S(1)}, s32[8,128]{1,0:T(8,128)S(1)}) custom-call(s32[40]{0:T(128)S(1)} %bitcast.6, s32[40]{0:T(128)S(1)} %bitcast.8, bf16[40,128,128]{2,1,0:T(8,128)(2,1)S(1)} %bitcast.4), custom_call_target="tpu_custom_call" | custom-call | tf_op jit(solution)/shard_map/gather/pallas_call | solution.py:232
  81.8 0.0 copy-done.5
  81.8 0.0 copy-done.3
  81.8 0.0 copy-done.1
  81.8 6.2 %multiply.1 = bf16[40,128,128]{2,1,0:T(8,128)(2,1)} custom-call(s32[40]{0:T(128)S(1)} %bitcast.7, s32[40]{0:T(128)S(1)} %bitcast.9, s32[8,128]{1,0:T(8,128)S(1)} %get-tuple-element.8.shifted_s, bf16[40,128,128]{2,1,0:T(8,128)(2,1)S(1)} %bitcast.5, bf16[40,128,128]{2,1,0:T(8,128)(2,1)S(1)} %get-tuple-element.9.shifted, ...), custom_call_target="tpu_custom_call" | custom-call | tf_op jit(solution)/shard_map/multiply/pallas_call | solution.py:337
Async XLA Ops:
  0.0 81.8 %copy-start.5 = (s32[1,1,40]{2,1,0:T(1,128)S(1)}, s32[1,1,40]{2,1,0:T(1,128)}, u32[]{:S(2)}) copy-start(s32[1,1,40]{2,1,0:T(1,128)} %param.5) | copy-start | bytes 484
  0.0 81.8 %copy-start.3 = (s32[1,1,40]{2,1,0:T(1,128)S(1)}, s32[1,1,40]{2,1,0:T(1,128)}, u32[]{:S(2)}) copy-start(s32[1,1,40]{2,1,0:T(1,128)} %param.4) | copy-start | bytes 484
  0.0 1.3 %copy-start = (bf16[1,1,40,128,128]{4,3,2,1,0:T(8,128)(2,1)S(1)}, bf16[1,1,40,128,128]{4,3,2,1,0:T(8,128)(2,1)}, u32[]{:S(2)}) copy-start(bf16[1,1,40,128,128]{4,3,2,1,0:T(8,128)(2,1)} %param.3) | copy-start | bytes 3932164
  1.3 0.7 copy-start.2
  2.0 0.7 copy-start.4
  2.7 79.2 %copy-start.1 = (bf16[1,1,40,128,128]{4,3,2,1,0:T(8,128)(2,1)S(1)}, bf16[1,1,40,128,128]{4,3,2,1,0:T(8,128)(2,1)}, u32[]{:S(2)}) copy-start(bf16[1,1,40,128,128]{4,3,2,1,0:T(8,128)(2,1)} %param.3) | copy-start | bytes 3932164

commit v2 on v1

v2 whole, which is shorter than its diff:
```python
import functools

import jax
import jax.numpy as jnp
from jax import lax
from jax.experimental import pallas as pl
from jax.experimental.pallas import tpu as pltpu
from jax.sharding import PartitionSpec as P

MESH = pl.DeviceIdType.MESH
BS = 128
BROW = 13
HALF = 20
SLOTS = 40
ROOM = 16
N_ROW = 32
N_COL = 16
PIECES = 4
PER = HALF // PIECES
PIECE_ROWS = PER * BS
CHUNKS = ((0, 320), (320, PIECE_ROWS))
ASIDE = (0,)
STRAIGHT = (1,)
ORDER = (1, 0)
MEETINGS = 2 * 178
GROUP = 4


def gather_kernel(
    partial,
    rows_s, cols_s, blocks,
    left, right, metas, flag,
    held, stage, packed, meta, below_meta, root_meta, order_v, order_s, need_v, need_s, onward, aside,
    chip_flags, z_flags, y_flags, flag_v,
    local_sem, root_sem, piece_sem, onward_sem, aside_sem, cross_sem, near_sem, x_sem, core_sem,
    shift_send, shift_recv, meta_send, meta_recv, flag_send, flag_recv,
):
    r, c = lax.axis_index("row"), lax.axis_index("col")
    y, zl = r // 8, r % 8
    zh, x, k = c // 8, (c // 2) % 4, c % 2
    z = zh * 8 + zl
    above, below = (r + 1) % N_ROW, (r + N_ROW - 1) % N_ROW

    def mirrored(row):
        return row + 8 * (3 - 2 * (row // 8))

    def home(row):
        return row // 16

    across = mirrored(r)
    across_below = (across + N_ROW - 1) % N_ROW
    first_root = c == r // 2
    second_root = c == below // 2
    first_panel, second_panel = k == 0, k == 1
    own_first = jnp.logical_and(first_root, first_panel)
    own_second = jnp.logical_and(second_root, second_panel)
    near = zh == home(r)
    far = jnp.logical_not(near)
    near_first = jnp.logical_and(first_panel, near)
    aside_first = jnp.logical_and(first_panel, far)
    near_second = jnp.logical_and(second_panel, zh == home(below))
    aside_second = jnp.logical_and(second_panel, zh == home(across_below))

    def at(x_of, k_of, zh_of=zh):
        return zh_of * 8 + x_of * 2 + k_of

    same, other = at(x, k), at(x, k, 1 - zh)
    ring = [(x + d) % 4 for d in (1, 3, 2)]
    chip_peers = [(r, zh * 8 + (x * 2 + k + d) % 8) for d in range(1, 8)]
    z_peers = [(y * 8 + (z + d) % 8, ((z + d) % 16) // 8 * 8 + x * 2 + k) for d in range(1, 16)]
    y_peers = [((y + d) % 4 * 8 + zl, c) for d in range(1, 4)]
    row_peers = [(r, (c + d) % N_COL) for d in range(1, N_COL)]
    barrier = pltpu.get_barrier_semaphore()

    def greet(row, col):
        pl.semaphore_signal(barrier, inc=1, device_id=(row, col), device_id_type=MESH)

    def greet_if(condition, row, col):
        @pl.when(condition)
        def _():
            greet(row, col)

    greet_if(jnp.logical_and(first_panel, far), r, other)
    greet_if(jnp.logical_and(first_panel, far), across, other)
    greet_if(jnp.logical_and(second_panel, far), above, other)
    greet_if(jnp.logical_and(second_panel, far), mirrored(above), other)
    greet(above, r // 2)
    greet_if(jnp.logical_not(first_root), r, r // 2)
    greet_if(jnp.logical_and(second_panel, near), above, same)
    greet(above, c)
    greet_if(jnp.logical_and(near_first, jnp.logical_not(own_first)), r, r // 2)
    greet_if(aside_first, across, across // 2)
    greet_if(jnp.logical_and(near_second, jnp.logical_not(own_second)), r, below // 2)
    greet_if(aside_second, across, across_below // 2)
    if partial:
        greet_if(jnp.logical_not(second_root), r, below // 2)
        greet(below, c)
        for peer in z_peers + y_peers + chip_peers:
            greet(*peer)
    greet(r, at(x, 1 - k))
    for x_of in ring:
        greet(r, at(x_of, k))

    is_root = jnp.logical_or(first_root, second_root)

    def fetch():
        return pltpu.make_async_copy(blocks, held, local_sem.at[0])

    if partial:
        fetch().start()
    else:
        pl.when(is_root)(lambda: fetch().start())

    lane = lax.broadcasted_iota(jnp.int32, (8, 128), 1)
    sub = lax.broadcasted_iota(jnp.int32, (8, 128), 0)

    def place(t, carry):
        n0, n1, own, order = carry
        a, b = rows_s[t], cols_s[t]
        half = jnp.where(b >= BROW, 1, 0)
        live = jnp.where(a >= 0, 1, 0)
        spot = jnp.where(a >= 0, jnp.where(b >= BROW, n1, n0), 127)
        own = jnp.where(lane == t, jnp.where(sub == 0, a, b), own)
        order = jnp.where(jnp.logical_and(lane == spot, sub == half), t, order)
        return n0 + live * (1 - half), n1 + live * half, own, order

    zero = jnp.zeros((8, 128), jnp.int32)
    _, _, own, order = lax.fori_loop(0, SLOTS, place, (jnp.int32(0), jnp.int32(0), zero - 1, zero))
    meta[...] = own

    @pl.when(is_root)
    def _():
        order_v[...] = order
        to_scalars = pltpu.make_async_copy(order_v, order_s, local_sem.at[1])
        to_scalars.start()
        to_scalars.wait()

    if partial:
        fetch().wait()
    else:
        pl.when(is_root)(lambda: fetch().wait())

    def pack(role, half):
        for i in range(PIECES):
            for j in range(PER):
                stage[role, i, j * BS:(j + 1) * BS, :] = held[jnp.clip(order_s[half, i * PER + j], 0, SLOTS - 1)].T

    @pl.when(first_root)
    def _():
        pack(0, r % 2)

    @pl.when(second_root)
    def _():
        pack(1, below % 2)

    def remote(src, dst, send, recv, row, col):
        return pltpu.make_async_remote_copy(
            src_ref=src, dst_ref=dst, send_sem=send, recv_sem=recv, device_id=(row, col), device_id_type=MESH
        )

    def chunk(ref, h):
        first, last = CHUNKS[h]
        return ref.at[pl.ds(first, last - first)]

    def pass_on(panel, i, h, send, row, col, source=None):
        here = chunk(left.at[panel, i], h)
        return remote(here if source is None else source, here, send, piece_sem.at[panel, i, h], row, col)

    def first_copy(i, h):
        return pass_on(0, i, h, root_sem.at[0, 0, i, h], r, at(i, 0), chunk(stage.at[0, i], h))

    def second_copy(i, h):
        return remote(
            chunk(stage.at[1, i], h), chunk(onward, h), root_sem.at[1, 0, i, h], onward_sem.at[h], r, at(i, 1)
        )

    def aside_copy(role, i, h):
        return remote(
            chunk(stage.at[role, i], h), chunk(aside, h), root_sem.at[role, 1, i, h], aside_sem.at[h], across, at(i, role)
        )

    def for_root_copies(do):
        def both(role, i, h, direct, own):
            if h in ASIDE:
                do(aside_copy(role, i, h))

            @pl.when(jnp.logical_not(jnp.logical_and(own, x == i)))
            def _():
                do(direct(i, h))

        @pl.when(first_root)
        def _():
            for h in ORDER:
                for i in range(PIECES):
                    both(0, i, h, first_copy, own_first)

        @pl.when(second_root)
        def _():
            for h in ORDER:
                for i in range(PIECES):
                    both(1, i, h, second_copy, own_second)

    def keep(condition, source, target, do):
        @pl.when(condition)
        def _():
            do(pltpu.make_async_copy(source, target, local_sem.at[2]))

    def keep_first(do):
        keep(own_first, stage.at[0, x], left.at[0, x], do)

    def keep_second(do):
        keep(own_second, stage.at[1, x], onward, do)

    def first_meta(peer):
        return remote(meta, metas.at[0], meta_send.at[0], meta_recv.at[0], *peer)

    def second_meta(peer):
        return remote(meta, metas.at[1], meta_send.at[1], meta_recv.at[1], *peer)

    def home_meta(peer):
        return remote(meta, root_meta, meta_send.at[4], meta_recv.at[4], *peer)

    shift_meta = remote(meta, metas.at[2], meta_send.at[2], meta_recv.at[2], below, c)
    if partial:
        upward_meta = remote(meta, below_meta, meta_send.at[3], meta_recv.at[3], above, c)

    def sent(n, send):
        many = z_flags.at[pl.ds(0, n)]
        remote(many, many, send, flag_recv.at[0], below, c).wait_send()

    slots = ROOM if partial else SLOTS
    parts = 2 if partial else 5

    def shift_copy(i):
        part = pl.ds(i * (slots // parts), slots // parts)
        source = packed if partial else blocks
        return remote(source.at[part], right.at[part], shift_send.at[i], shift_recv.at[i], below, c)

    def straight_first(h):
        return pass_on(0, x, h, cross_sem.at[h], r, other)

    def straight_second(h):
        return pass_on(1, x, h, cross_sem.at[h], below, other, chunk(onward, h))

    def to_near(h):
        return pass_on(1, x, h, near_sem.at[h], below, same, chunk(onward, h))

    def from_aside(role, h):
        return pass_on(role, x, h, cross_sem.at[h], across if role == 0 else across_below, other, chunk(aside, h))

    def x_copy(n, h):
        return pass_on(k, x, h, x_sem.at[n, h], r, at(ring[n], k))

    def core_copy(n, i, h):
        return pass_on(k, i, h, core_sem.at[n, h], r, at(x, 1 - k))

    def arrived(panel, i, h):
        pass_on(panel, i, h, core_sem.at[0, 0], r, at(x, 1 - k)).wait_recv()

    def landed(ref, h, sem):
        remote(chunk(ref, h), chunk(ref, h), core_sem.at[0, 0], sem.at[h], r, at(x, 1 - k)).wait_recv()

    def amount(condition, n):
        return jnp.where(condition, n, 0)

    sends = (
        5
        + amount(first_root, 8 + 15) - amount(own_first, 1)
        + amount(second_root, 8 + 16) - amount(own_second, 1)
        + amount(near_first, 1) + amount(aside_first, 1) + amount(near_second, 2) + amount(aside_second, 1)
    )
    if partial:
        sends = sends + 1 + 25 + amount(second_root, 15)
    pl.semaphore_wait(barrier, sends)

    if partial:
        upward_meta.start()

        @pl.when(second_root)
        def _():
            for peer in row_peers:
                home_meta(peer).start()
            root_meta[...] = meta[...]

    for_root_copies(lambda copy: copy.start())
    keep_first(lambda copy: copy.start())
    keep_second(lambda copy: copy.start())
    shift_meta.start()

    if not partial:
        for i in range(parts):
            shift_copy(i).start()

    def own_meta():
        return pltpu.make_async_copy(meta, metas.at[0], local_sem.at[1])

    @pl.when(first_root)
    def _():
        for peer in row_peers:
            first_meta(peer).start()
        own_meta().start()

    @pl.when(second_root)
    def _():
        for col in range(N_COL):
            second_meta((below, col)).start()

    keep_first(lambda copy: copy.wait())
    keep_second(lambda copy: copy.wait())

    def spread(h):
        for n in range(3):
            x_copy(n, h).start()
        core_copy(0, x, h).start()

    @pl.when(near_first)
    def _():
        for h in ORDER:
            @pl.when(jnp.logical_not(own_first))
            def _():
                arrived(0, x, h)

            if h in STRAIGHT:
                straight_first(h).start()
            spread(h)

    @pl.when(aside_first)
    def _():
        for h in ASIDE:
            landed(aside, h, aside_sem)
            from_aside(0, h).start()

    @pl.when(near_second)
    def _():
        for h in ORDER:
            @pl.when(jnp.logical_not(own_second))
            def _():
                landed(onward, h, onward_sem)

            if h in STRAIGHT:
                straight_second(h).start()
            to_near(h).start()

    @pl.when(aside_second)
    def _():
        for h in ASIDE:
            landed(aside, h, aside_sem)
            from_aside(1, h).start()

    def send_flags(peers, buffer, me, n):
        buffer[me] = flag_v[n]
        for peer in peers:
            remote(flag_v.at[n], buffer.at[me], flag_send.at[n], flag_recv.at[n], *peer).start()

    def join_flags(buffer, count, n):
        others = buffer.at[pl.ds(0, count - 1)]
        remote(others, others, flag_send.at[n], flag_recv.at[n], below, c).wait_recv()
        joined = buffer[0]
        for i in range(1, count):
            joined = jnp.maximum(joined, buffer[i])
        return joined

    if partial:
        upward_meta.wait_recv()

        @pl.when(jnp.logical_not(second_root))
        def _():
            home_meta(row_peers[0]).wait_recv()

        wide_lane = lax.broadcasted_iota(jnp.int32, (SLOTS, 128), 1)
        wide_sub = lax.broadcasted_iota(jnp.int32, (SLOTS, 128), 0)

        def down(values):
            return jnp.sum(jnp.where(wide_lane == wide_sub, values, 0), axis=1, keepdims=True)

        def bits(rows, valid):
            return jnp.where(valid, jnp.left_shift(1, jnp.maximum(rows, 0)), 0)

        def union(keys, masks, wanted):
            return jnp.sum(jnp.where(down(keys) == wanted, down(masks), 0), axis=0, keepdims=True)

        line, column = own[0:1, :], own[1:2, :]
        theirs, half_meta = below_meta[...], root_meta[...]
        left_line, left_column = half_meta[0:1, :], half_meta[1:2, :] - BROW * (below % 2)
        in_half = jnp.logical_and(left_line >= 0, jnp.logical_and(left_column >= 0, left_column < BROW))
        by_line = union(left_line, bits(jnp.minimum(left_column, BROW), in_half), line)
        by_column = union(theirs[1:2, :], bits(theirs[0:1, :], theirs[0:1, :] >= 0), column)
        needed = jnp.logical_and(line >= 0, jnp.bitwise_and(by_line, by_column) != 0)
        count = jnp.where(needed, 1, 0)
        rank = jnp.sum(jnp.where(wide_sub < wide_lane, down(count), 0), axis=0, keepdims=True)
        spot_sub = lax.broadcasted_iota(jnp.int32, (ROOM, 128), 0)
        spot_lane = lax.broadcasted_iota(jnp.int32, (ROOM, 128), 1)
        chosen = jnp.logical_and(needed, rank == spot_sub)
        slot = jnp.sum(jnp.where(chosen, spot_lane, 0), axis=1, keepdims=True)
        need_v[...] = jnp.broadcast_to(slot, (ROOM, 128))
        needs = pltpu.make_async_copy(need_v, need_s, local_sem.at[3])
        needs.start()
        total = jnp.sum(count, axis=1, keepdims=True)
        flag_v[0] = jnp.broadcast_to(jnp.where(total > ROOM, 1, 0), (8, 128))
        needs.wait()
        for s in range(ROOM):
            packed[s] = held[jnp.clip(need_s[s, 0], 0, SLOTS - 1)]
        for i in range(parts):
            shift_copy(i).start()
        send_flags(chip_peers, chip_flags, x * 2 + k, 0)

    if partial:
        flag_v[1] = join_flags(chip_flags, 8, 0)
        send_flags(z_peers, z_flags, z, 1)

    @pl.when(jnp.logical_not(near_first))
    def _():
        for h in ORDER:
            arrived(k, x, h)
            spread(h)

    if partial:
        flag_v[2] = join_flags(z_flags, 16, 1)
        send_flags(y_peers, y_flags, y, 2)

    for h in ORDER:
        for n in range(3):
            arrived(k, ring[n], h)
            core_copy(1 + n, ring[n], h).start()

    for h in ORDER:
        for i in range(PIECES):
            arrived(1 - k, i, h)

    if partial:
        flag[0, 0] = jnp.max(join_flags(y_flags, 4, 2))
        sent(7, flag_send.at[0])
        sent(15, flag_send.at[1])
        sent(3, flag_send.at[2])
    else:
        flag[0, 0] = 0

    for_root_copies(lambda copy: copy.wait_send())

    @pl.when(first_root)
    def _():
        own_meta().wait()
        sent(15, meta_send.at[0])

    @pl.when(jnp.logical_not(first_root))
    def _():
        first_meta(row_peers[0]).wait_recv()

    @pl.when(second_root)
    def _():
        sent(16, meta_send.at[1])

    second_meta((below, c)).wait_recv()
    shift_meta.wait()
    if partial:
        upward_meta.wait_send()

        @pl.when(second_root)
        def _():
            sent(15, meta_send.at[4])

    @pl.when(near_first)
    def _():
        for h in STRAIGHT:
            straight_first(h).wait_send()

    @pl.when(near_second)
    def _():
        for h in STRAIGHT:
            straight_second(h).wait_send()
        for h in ORDER:
            to_near(h).wait_send()

    @pl.when(aside_first)
    def _():
        for h in ASIDE:
            from_aside(0, h).wait_send()

    @pl.when(aside_second)
    def _():
        for h in ASIDE:
            from_aside(1, h).wait_send()

    for h in ORDER:
        for n in range(3):
            x_copy(n, h).wait_send()
        core_copy(0, x, h).wait_send()
        for n in range(3):
            core_copy(1 + n, ring[n], h).wait_send()
    for i in range(parts):
        shift_copy(i).wait()


def gather(rows, cols, blocks, partial):
    any_space = pl.BlockSpec(memory_space=pl.ANY)
    scalars = pl.BlockSpec(memory_space=pltpu.SMEM)
    dma = pltpu.SemaphoreType.DMA
    tile = (8, 128)
    hops = len(CHUNKS)
    return pl.pallas_call(
        functools.partial(gather_kernel, partial),
        name="gather_needed" if partial else "gather_all",
        out_shape=(
            jax.ShapeDtypeStruct((2, PIECES, PIECE_ROWS, BS), jnp.bfloat16),
            jax.ShapeDtypeStruct((ROOM if partial else SLOTS, BS, BS), jnp.bfloat16),
            jax.ShapeDtypeStruct((3, *tile), jnp.int32),
            jax.ShapeDtypeStruct((1, 1), jnp.int32),
        ),
        in_specs=[scalars, scalars, any_space],
        out_specs=(any_space, any_space, any_space, scalars),
        scratch_shapes=[
            pltpu.VMEM((SLOTS, BS, BS), jnp.bfloat16),
            pltpu.VMEM((2, PIECES, PIECE_ROWS, BS), jnp.bfloat16),
            pltpu.VMEM((ROOM, BS, BS), jnp.bfloat16),
            pltpu.VMEM(tile, jnp.int32),
            pltpu.VMEM(tile, jnp.int32),
            pltpu.VMEM(tile, jnp.int32),
            pltpu.VMEM(tile, jnp.int32),
            pltpu.SMEM(tile, jnp.int32),
            pltpu.VMEM((ROOM, 128), jnp.int32),
            pltpu.SMEM((ROOM, 128), jnp.int32),
            pltpu.VMEM((PIECE_ROWS, BS), jnp.bfloat16),
            pltpu.VMEM((PIECE_ROWS, BS), jnp.bfloat16),
            pltpu.VMEM((8, *tile), jnp.int32),
            pltpu.VMEM((16, *tile), jnp.int32),
            pltpu.VMEM((4, *tile), jnp.int32),
            pltpu.VMEM((3, *tile), jnp.int32),
            dma((4,)),
            dma((2, 2, PIECES, hops)),
            dma((2, PIECES, hops)),
            dma((hops,)),
            dma((hops,)),
            dma((hops,)),
            dma((hops,)),
            dma((3, hops)),
            dma((PIECES, hops)),
            dma((5,)),
            dma((5,)),
            dma((5,)),
            dma((5,)),
            dma((3,)),
            dma((3,)),
        ],
        compiler_params=pltpu.CompilerParams(
            collective_id=0 if partial else 1, has_side_effects=True, vmem_limit_bytes=GATHER_MIB * 1024 * 1024
        ),
    )(rows, cols, blocks)


GATHER_MIB = 62
MULTIPLY_MIB = 62


def multiply_kernel(
    partial,
    rows_s, cols_s, metas_s, blocks, right, left, out,
    left_mask, right_mask, line_mask, left_slot, right_slot, where_s, slot_s, count_s,
    zeros, left_v, right_v, total, done, zero_sem, load_sem, store_sem,
):
    half = lax.axis_index("row") % 2
    zeros[...] = jnp.zeros_like(zeros)
    clear = pltpu.make_async_copy(zeros, out, zero_sem)
    clear.start()
    for i in range(16):
        line_mask[i] = 0
    for i in range(32):
        left_mask[i] = 0
    for i in range(64):
        right_mask[i] = 0
    count_s[0] = 0
    count_s[1] = 0

    def put(mask, key, live, bit):
        mask[key] = mask[key] | jnp.where(live, jnp.left_shift(1, jnp.maximum(bit, 0)), 0)

    def tables(t, carry):
        found = list(carry)
        a, b = rows_s[t], cols_s[t]
        live = a >= 0
        put(right_mask, jnp.where(live, b, 31), live, a)
        right_slot[jnp.where(live, b * 16 + a, 511)] = t
        for p in range(2):
            m, i = metas_s[p, 0, t], metas_s[p, 1, t] - BROW * half
            live = jnp.logical_and(m >= 0, jnp.logical_and(i >= 0, i < BROW))
            put(left_mask, jnp.where(live, p * 16 + i, 15), live, m)
            left_slot[jnp.where(live, p * 256 + i * 16 + m, 255)] = found[p]
            found[p] = found[p] + jnp.where(live, 1, 0)
            if p == 1:
                put(line_mask, jnp.where(live, m, 15), live, i)
        return tuple(found)

    lax.fori_loop(0, SLOTS, tables, (jnp.int32(0), jnp.int32(0)))

    def second_table(t, found):
        m, b = metas_s[2, 0, t], metas_s[2, 1, t]
        live = m >= 0
        if partial:
            live = jnp.logical_and(live, (line_mask[jnp.where(live, m, 15)] & right_mask[jnp.where(live, b, 31)]) != 0)
            live = jnp.logical_and(live, found < ROOM)
        put(right_mask, jnp.where(live, 32 + b, 63), live, m)
        right_slot[jnp.where(live, 512 + b * 16 + m, 1023)] = found if partial else t
        return found + jnp.where(live, 1, 0)

    lax.fori_loop(0, SLOTS, second_table, jnp.int32(0))

    def load(p, i, m, b, t):
        n = jnp.minimum(count_s[0], MEETINGS - 1)
        j = jnp.minimum(left_slot[p * 256 + i * 16 + m], HALF - 1)
        piece = j // PER
        start = pl.multiple_of((j - piece * PER) * BS, BS)
        source = (blocks, right)[p]
        pltpu.make_async_copy(left.at[p, piece, pl.ds(start, BS)], left_v.at[n], load_sem.at[0]).start()
        slot = jnp.minimum(right_slot[p * 512 + b * 16 + m], source.shape[0] - 1)
        pltpu.make_async_copy(source.at[slot], right_v.at[n], load_sem.at[1]).start()
        where_s[n] = t
        count_s[0] = n + 1

    @pl.loop(0, SLOTS)
    def _(t):
        a, b = rows_s[t], cols_s[t]

        @pl.when(a >= 0)
        def _():
            meet = [left_mask[p * 16 + a] & right_mask[p * 32 + b] for p in range(2)]

            @pl.when((meet[0] | meet[1]) != 0)
            def _():
                slot_s[count_s[1]] = t
                count_s[1] = count_s[1] + 1
                total[t] = jnp.zeros_like(total[t])
                for p in range(2):
                    @pl.when(meet[p] != 0)
                    def _():
                        @pl.loop(0, BROW)
                        def _(m):
                            @pl.when(((meet[p] >> m) & 1) != 0)
                            def _():
                                load(p, a, m, b, t)

    n, slots = count_s[0], count_s[1]
    for u in range(GROUP):
        where_s[n + u] = SLOTS

    @pl.loop(0, n)
    def _(i):
        pltpu.make_async_copy(blocks.at[0], left_v.at[0], load_sem.at[0]).wait()
        pltpu.make_async_copy(blocks.at[0], right_v.at[0], load_sem.at[1]).wait()

    @pl.loop(0, (n + GROUP - 1) // GROUP)
    def _(g):
        products = [
            jnp.dot(left_v[g * GROUP + u], right_v[g * GROUP + u], preferred_element_type=jnp.float32)
            for u in range(GROUP)
        ]
        for u in range(GROUP):
            t = where_s[g * GROUP + u]
            total[t] = total[t] + products[u]

    clear.wait()

    @pl.loop(0, slots)
    def _(i):
        t = slot_s[i]
        done[i] = total[t].astype(jnp.bfloat16)
        pltpu.make_async_copy(done.at[i], out.at[t], store_sem).start()

    @pl.loop(0, slots)
    def _(i):
        pltpu.make_async_copy(done.at[0], out.at[0], store_sem).wait()


def multiply(rows, cols, metas, blocks, right, left, partial):
    scalars = pl.BlockSpec(memory_space=pltpu.SMEM)
    any_space = pl.BlockSpec(memory_space=pl.ANY)
    room = MEETINGS + GROUP
    return pl.pallas_call(
        functools.partial(multiply_kernel, partial),
        name="multiply",
        out_shape=jax.ShapeDtypeStruct((SLOTS, BS, BS), jnp.bfloat16),
        in_specs=[scalars, scalars, scalars, any_space, any_space, any_space],
        out_specs=any_space,
        scratch_shapes=[
            pltpu.SMEM((32,), jnp.int32),
            pltpu.SMEM((64,), jnp.int32),
            pltpu.SMEM((16,), jnp.int32),
            pltpu.SMEM((512,), jnp.int32),
            pltpu.SMEM((1024,), jnp.int32),
            pltpu.SMEM((room,), jnp.int32),
            pltpu.SMEM((SLOTS,), jnp.int32),
            pltpu.SMEM((2,), jnp.int32),
            pltpu.VMEM((SLOTS, BS, BS), jnp.bfloat16),
            pltpu.VMEM((room, BS, BS), jnp.bfloat16),
            pltpu.VMEM((room, BS, BS), jnp.bfloat16),
            pltpu.VMEM((SLOTS + 1, BS, BS), jnp.float32),
            pltpu.VMEM((SLOTS, BS, BS), jnp.bfloat16),
            pltpu.SemaphoreType.DMA,
            pltpu.SemaphoreType.DMA((2,)),
            pltpu.SemaphoreType.DMA,
        ],
        compiler_params=pltpu.CompilerParams(vmem_limit_bytes=MULTIPLY_MIB * 1024 * 1024),
    )(rows, cols, metas, blocks, right, left)


def product(rows, cols, blocks, partial):
    left, right, metas, flag = gather(rows, cols, blocks, partial)
    return multiply(rows, cols, metas, blocks, right, left, partial), flag


def shards(blocks, block_rows, block_cols):
    blocks, rows, cols = blocks[0, 0], block_rows[0, 0], block_cols[0, 0]
    result, flag = product(rows, cols, blocks, True)
    result = lax.cond(flag[0, 0] > 0, lambda: product(rows, cols, blocks, False)[0], lambda: result)
    return result[None, None]


def solution(mesh):
    return jax.shard_map(
        shards,
        mesh=mesh,
        in_specs=(P("row", "col", None, None, None), P("row", "col", None), P("row", "col", None)),
        out_specs=P("row", "col", None, None, None),
        check_vma=False,
    )
```

time: 88.2 us -> 69.9 us (0.79)
  the two profiles are of different devices: /device:TPU:223 before, /device:TPU:29 now
where the time goes in v2:
time: 69.9 us; the launch traced here: 69.6 us
  Pallas kernels  68.9 us (99%)
    pallas_call x1, Pallas kernels, gather(): pl.pallas_call(functools.partial(gather_kernel, partial), name='gather_ne...  59.7 us
    pallas_call x1, Pallas kernels, multiply(): pl.pallas_call(functools.partial(multiply_kernel, partial), name='multipl...  9.24 us

profile of v2, /device:TPU:29, one launch (start us, length us, event | category | flops | bytes accessed | tf_op | source)
XLA Modules:
  0.0 69.6 jit_solution(13412454130988081683)
XLA Ops:
  0.0 0.0 copy-start.2
  0.0 0.0 copy-start.1
  0.0 0.0 copy-start
  0.0 59.7 %gather_needed.1 = (bf16[2,4,640,128]{3,2,1,0:T(8,128)(2,1)}, bf16[16,128,128]{2,1,0:T(8,128)(2,1)}, s32[3,8,128]{2,1,0:T(8,128)}, s32[1,1]{1,0:T(1,128)}) custom-call(s32[40]{0:T(128)} %bitcast.11, s32[40]{0:T(128)} %bitcast.14, bf16[40,128,128]{2,1,0:T(8,128)(2,1)} %bitcast.6), custom_call_target="tpu_custom_call" | custom-call | tf_op jit(solution)/shard_map/gather_needed/pallas_call | solution.py:500
  60.3 0.0 copy-done.2
  60.3 0.0 copy-done.1
  60.3 0.0 copy-done
  60.3 9.2 %multiply.3 = bf16[40,128,128]{2,1,0:T(8,128)(2,1)} custom-call(s32[40]{0:T(128)S(1)} %bitcast.12, s32[40]{0:T(128)S(1)} %bitcast.15, s32[3,8,128]{2,1,0:T(8,128)} %get-tuple-element.28.metas_s, bf16[40,128,128]{2,1,0:T(8,128)(2,1)S(1)} %bitcast.7, bf16[16,128,128]{2,1,0:T(8,128)(2,1)} %get-tuple-element.29.right, ...), custom_call_target="tpu_custom_call" | custom-call | tf_op jit(solution)/shard_map/multiply/pallas_call | solution.py:676
  (1 shorter events, 0.0 us)
Async XLA Ops:
  0.0 60.3 %copy-start.2 = (s32[1,1,40]{2,1,0:T(1,128)S(1)}, s32[1,1,40]{2,1,0:T(1,128)}, u32[]{:S(2)}) copy-start(s32[1,1,40]{2,1,0:T(1,128)} %param.7) | copy-start | bytes 484
  0.0 60.3 %copy-start.1 = (s32[1,1,40]{2,1,0:T(1,128)S(1)}, s32[1,1,40]{2,1,0:T(1,128)}, u32[]{:S(2)}) copy-start(s32[1,1,40]{2,1,0:T(1,128)} %param.6) | copy-start | bytes 484
  0.0 60.3 %copy-start = (bf16[1,1,40,128,128]{4,3,2,1,0:T(8,128)(2,1)S(1)}, bf16[1,1,40,128,128]{4,3,2,1,0:T(8,128)(2,1)}, u32[]{:S(2)}) copy-start(bf16[1,1,40,128,128]{4,3,2,1,0:T(8,128)(2,1)} %param.5) | copy-start | bytes 3932164

commit v3 on v2

--- a/solution.py
+++ b/solution.py
@@ -29,8 +29,8 @@
 def gather_kernel(
     partial,
     rows_s, cols_s, blocks,
-    left, right, metas, flag,
-    held, stage, packed, meta, below_meta, root_meta, order_v, order_s, need_v, need_s, onward, aside,
+    left, right, plan, flag,
+    metas, held, stage, packed, meta, below_meta, root_meta, order_v, order_s, need_v, need_s, onward, aside,
     chip_flags, z_flags, y_flags, flag_v,
     local_sem, root_sem, piece_sem, onward_sem, aside_sem, cross_sem, near_sem, x_sem, core_sem,
     shift_send, shift_recv, meta_send, meta_recv, flag_send, flag_recv,
@@ -188,15 +188,14 @@
             def _():
                 do(direct(i, h))
 
-        @pl.when(first_root)
-        def _():
-            for h in ORDER:
+        for h in ORDER:
+            @pl.when(first_root)
+            def _():
                 for i in range(PIECES):
                     both(0, i, h, first_copy, own_first)
 
-        @pl.when(second_root)
-        def _():
-            for h in ORDER:
+            @pl.when(second_root)
+            def _():
                 for i in range(PIECES):
                     both(1, i, h, second_copy, own_second)
 
@@ -291,14 +290,11 @@
         for i in range(parts):
             shift_copy(i).start()
 
-    def own_meta():
-        return pltpu.make_async_copy(meta, metas.at[0], local_sem.at[1])
-
     @pl.when(first_root)
     def _():
         for peer in row_peers:
             first_meta(peer).start()
-        own_meta().start()
+        metas[0] = meta[...]
 
     @pl.when(second_root)
     def _():
@@ -360,6 +356,34 @@
             joined = jnp.maximum(joined, buffer[i])
         return joined
 
+    wide_lane = lax.broadcasted_iota(jnp.int32, (SLOTS, 128), 1)
+    wide_sub = lax.broadcasted_iota(jnp.int32, (SLOTS, 128), 0)
+
+    line, column = own[0:1, :], own[1:2, :]
+
+    def down(values):
+        return jnp.sum(jnp.where(wide_lane == wide_sub, values, 0), axis=1, keepdims=True)
+
+    def bits(rows, valid):
+        return jnp.where(valid, jnp.left_shift(1, jnp.maximum(rows, 0)), 0)
+
+    def union(keys, masks, wanted):
+        return jnp.sum(jnp.where(down(keys) == wanted, down(masks), 0), axis=0, keepdims=True)
+
+    def rank(chosen):
+        return jnp.sum(jnp.where(wide_sub < wide_lane, down(jnp.where(chosen, 1, 0)), 0), axis=0, keepdims=True)
+
+    def left_half(coords, which):
+        lines, columns = coords[0:1, :], coords[1:2, :] - BROW * which
+        inside = jnp.logical_and(lines >= 0, jnp.logical_and(columns >= 0, columns < BROW))
+        return lines, jnp.where(inside, columns, -1), inside
+
+    def needs_of(lines, columns, half_coords, output_lines, output_columns):
+        left_lines, left_columns, inside = half_coords
+        by_line = union(left_lines, bits(left_columns, inside), lines)
+        by_column = union(output_columns, bits(output_lines, output_lines >= 0), columns)
+        return jnp.logical_and(lines >= 0, jnp.bitwise_and(by_line, by_column) != 0)
+
     if partial:
         upward_meta.wait_recv()
 
@@ -367,35 +391,16 @@
         def _():
             home_meta(row_peers[0]).wait_recv()
 
-        wide_lane = lax.broadcasted_iota(jnp.int32, (SLOTS, 128), 1)
-        wide_sub = lax.broadcasted_iota(jnp.int32, (SLOTS, 128), 0)
-
-        def down(values):
-            return jnp.sum(jnp.where(wide_lane == wide_sub, values, 0), axis=1, keepdims=True)
-
-        def bits(rows, valid):
-            return jnp.where(valid, jnp.left_shift(1, jnp.maximum(rows, 0)), 0)
-
-        def union(keys, masks, wanted):
-            return jnp.sum(jnp.where(down(keys) == wanted, down(masks), 0), axis=0, keepdims=True)
-
-        line, column = own[0:1, :], own[1:2, :]
-        theirs, half_meta = below_meta[...], root_meta[...]
-        left_line, left_column = half_meta[0:1, :], half_meta[1:2, :] - BROW * (below % 2)
-        in_half = jnp.logical_and(left_line >= 0, jnp.logical_and(left_column >= 0, left_column < BROW))
-        by_line = union(left_line, bits(jnp.minimum(left_column, BROW), in_half), line)
-        by_column = union(theirs[1:2, :], bits(theirs[0:1, :], theirs[0:1, :] >= 0), column)
-        needed = jnp.logical_and(line >= 0, jnp.bitwise_and(by_line, by_column) != 0)
-        count = jnp.where(needed, 1, 0)
-        rank = jnp.sum(jnp.where(wide_sub < wide_lane, down(count), 0), axis=0, keepdims=True)
+        theirs = below_meta[...]
+        needed = needs_of(line, column, left_half(root_meta[...], below % 2), theirs[0:1, :], theirs[1:2, :])
         spot_sub = lax.broadcasted_iota(jnp.int32, (ROOM, 128), 0)
         spot_lane = lax.broadcasted_iota(jnp.int32, (ROOM, 128), 1)
-        chosen = jnp.logical_and(needed, rank == spot_sub)
+        chosen = jnp.logical_and(needed, rank(needed) == spot_sub)
         slot = jnp.sum(jnp.where(chosen, spot_lane, 0), axis=1, keepdims=True)
         need_v[...] = jnp.broadcast_to(slot, (ROOM, 128))
         needs = pltpu.make_async_copy(need_v, need_s, local_sem.at[3])
         needs.start()
-        total = jnp.sum(count, axis=1, keepdims=True)
+        total = jnp.sum(jnp.where(needed, 1, 0), axis=1, keepdims=True)
         flag_v[0] = jnp.broadcast_to(jnp.where(total > ROOM, 1, 0), (8, 128))
         needs.wait()
         for s in range(ROOM):
@@ -423,6 +428,40 @@
             arrived(k, ring[n], h)
             core_copy(1 + n, ring[n], h).start()
 
+    @pl.when(jnp.logical_not(first_root))
+    def _():
+        first_meta(row_peers[0]).wait_recv()
+
+    second_meta((below, c)).wait_recv()
+    shift_meta.wait_recv()
+    halves = [left_half(metas[p], r % 2) for p in range(2)]
+    shift_line, shift_column = metas[2, 0:1, :], metas[2, 1:2, :]
+    if partial:
+        present = needs_of(shift_line, shift_column, halves[1], line, column)
+        position = jnp.minimum(rank(present), ROOM - 1)
+    else:
+        present = shift_line >= 0
+        position = lane[0:1, :]
+    entries = []
+    for p, (lines, columns) in enumerate(((line, column), (shift_line, shift_column))):
+        left_lines, left_columns, inside = halves[p]
+        meet = jnp.bitwise_and(
+            union(left_columns, bits(left_lines, inside), line), union(columns, bits(lines, lines >= 0), column)
+        )
+        entries.append(jnp.where(line >= 0, meet, 0))
+        entries.append(jnp.where(inside, p * 256 + left_columns * 16 + left_lines, 255))
+        entries.append(jnp.minimum(rank(inside), HALF - 1))
+    entries.append(jnp.where(line >= 0, column * 16 + line, 511))
+    entries.append(jnp.where(present, 512 + shift_column * 16 + shift_line, 1023))
+    entries.append(position)
+    entries.append(jnp.maximum(line, 0) * 16)
+    entries.append(jnp.maximum(column, 0) * 16)
+    sub16 = lax.broadcasted_iota(jnp.int32, (16, 128), 0)
+    table = jnp.zeros((16, 128), jnp.int32)
+    for i, entry in enumerate(entries):
+        table = jnp.where(sub16 == i, entry, table)
+    plan[...] = table
+
     for h in ORDER:
         for i in range(PIECES):
             arrived(1 - k, i, h)
@@ -439,19 +478,13 @@
 
     @pl.when(first_root)
     def _():
-        own_meta().wait()
         sent(15, meta_send.at[0])
 
-    @pl.when(jnp.logical_not(first_root))
-    def _():
-        first_meta(row_peers[0]).wait_recv()
-
     @pl.when(second_root)
     def _():
         sent(16, meta_send.at[1])
 
-    second_meta((below, c)).wait_recv()
-    shift_meta.wait()
+    shift_meta.wait_send()
     if partial:
         upward_meta.wait_send()
 
@@ -503,12 +536,13 @@
         out_shape=(
             jax.ShapeDtypeStruct((2, PIECES, PIECE_ROWS, BS), jnp.bfloat16),
             jax.ShapeDtypeStruct((ROOM if partial else SLOTS, BS, BS), jnp.bfloat16),
-            jax.ShapeDtypeStruct((3, *tile), jnp.int32),
+            jax.ShapeDtypeStruct((16, 128), jnp.int32),
             jax.ShapeDtypeStruct((1, 1), jnp.int32),
         ),
         in_specs=[scalars, scalars, any_space],
-        out_specs=(any_space, any_space, any_space, scalars),
+        out_specs=(any_space, any_space, pl.BlockSpec(memory_space=pltpu.VMEM), scalars),
         scratch_shapes=[
+            pltpu.VMEM((3, *tile), jnp.int32),
             pltpu.VMEM((SLOTS, BS, BS), jnp.bfloat16),
             pltpu.VMEM((2, PIECES, PIECE_ROWS, BS), jnp.bfloat16),
             pltpu.VMEM((ROOM, BS, BS), jnp.bfloat16),
@@ -551,91 +585,59 @@
 MULTIPLY_MIB = 62
 
 
+MEET, LEFT_CELL, LEFT_PLACE = (0, 3), (1, 4), (2, 5)
+OWN_CELL, SHIFT_CELL, SHIFT_PLACE, LEFT_BASE, RIGHT_BASE = 6, 7, 8, 9, 10
+LOWEST = 0x09AF
+
+
 def multiply_kernel(
-    partial,
-    rows_s, cols_s, metas_s, blocks, right, left, out,
-    left_mask, right_mask, line_mask, left_slot, right_slot, where_s, slot_s, count_s,
+    plan, blocks, right, left, out,
+    left_slot, right_slot, bit_s, where_s, slot_s, count_s,
     zeros, left_v, right_v, total, done, zero_sem, load_sem, store_sem,
 ):
-    half = lax.axis_index("row") % 2
     zeros[...] = jnp.zeros_like(zeros)
     clear = pltpu.make_async_copy(zeros, out, zero_sem)
     clear.start()
     for i in range(16):
-        line_mask[i] = 0
-    for i in range(32):
-        left_mask[i] = 0
-    for i in range(64):
-        right_mask[i] = 0
+        bit_s[(LOWEST << i & 0xFFFF) >> 12] = i
     count_s[0] = 0
     count_s[1] = 0
 
-    def put(mask, key, live, bit):
-        mask[key] = mask[key] | jnp.where(live, jnp.left_shift(1, jnp.maximum(bit, 0)), 0)
-
-    def tables(t, carry):
-        found = list(carry)
-        a, b = rows_s[t], cols_s[t]
-        live = a >= 0
-        put(right_mask, jnp.where(live, b, 31), live, a)
-        right_slot[jnp.where(live, b * 16 + a, 511)] = t
+    @pl.loop(0, SLOTS, unroll=8)
+    def _(t):
         for p in range(2):
-            m, i = metas_s[p, 0, t], metas_s[p, 1, t] - BROW * half
-            live = jnp.logical_and(m >= 0, jnp.logical_and(i >= 0, i < BROW))
-            put(left_mask, jnp.where(live, p * 16 + i, 15), live, m)
-            left_slot[jnp.where(live, p * 256 + i * 16 + m, 255)] = found[p]
-            found[p] = found[p] + jnp.where(live, 1, 0)
-            if p == 1:
-                put(line_mask, jnp.where(live, m, 15), live, i)
-        return tuple(found)
-
-    lax.fori_loop(0, SLOTS, tables, (jnp.int32(0), jnp.int32(0)))
-
-    def second_table(t, found):
-        m, b = metas_s[2, 0, t], metas_s[2, 1, t]
-        live = m >= 0
-        if partial:
-            live = jnp.logical_and(live, (line_mask[jnp.where(live, m, 15)] & right_mask[jnp.where(live, b, 31)]) != 0)
-            live = jnp.logical_and(live, found < ROOM)
-        put(right_mask, jnp.where(live, 32 + b, 63), live, m)
-        right_slot[jnp.where(live, 512 + b * 16 + m, 1023)] = found if partial else t
-        return found + jnp.where(live, 1, 0)
-
-    lax.fori_loop(0, SLOTS, second_table, jnp.int32(0))
-
-    def load(p, i, m, b, t):
+            left_slot[plan[LEFT_CELL[p], t]] = plan[LEFT_PLACE[p], t]
+        right_slot[plan[OWN_CELL, t]] = t
+        right_slot[plan[SHIFT_CELL, t]] = plan[SHIFT_PLACE, t]
+
+    def load(p, m, t):
         n = jnp.minimum(count_s[0], MEETINGS - 1)
-        j = jnp.minimum(left_slot[p * 256 + i * 16 + m], HALF - 1)
+        j = jnp.clip(left_slot[p * 256 + plan[LEFT_BASE, t] + m], 0, HALF - 1)
         piece = j // PER
         start = pl.multiple_of((j - piece * PER) * BS, BS)
         source = (blocks, right)[p]
+        slot = jnp.clip(right_slot[p * 512 + plan[RIGHT_BASE, t] + m], 0, source.shape[0] - 1)
         pltpu.make_async_copy(left.at[p, piece, pl.ds(start, BS)], left_v.at[n], load_sem.at[0]).start()
-        slot = jnp.minimum(right_slot[p * 512 + b * 16 + m], source.shape[0] - 1)
         pltpu.make_async_copy(source.at[slot], right_v.at[n], load_sem.at[1]).start()
         where_s[n] = t
         count_s[0] = n + 1
 
     @pl.loop(0, SLOTS)
     def _(t):
-        a, b = rows_s[t], cols_s[t]
-
-        @pl.when(a >= 0)
+        meet = [plan[MEET[p], t] for p in range(2)]
+
+        @pl.when((meet[0] | meet[1]) != 0)
         def _():
-            meet = [left_mask[p * 16 + a] & right_mask[p * 32 + b] for p in range(2)]
-
-            @pl.when((meet[0] | meet[1]) != 0)
-            def _():
-                slot_s[count_s[1]] = t
-                count_s[1] = count_s[1] + 1
-                total[t] = jnp.zeros_like(total[t])
-                for p in range(2):
-                    @pl.when(meet[p] != 0)
-                    def _():
-                        @pl.loop(0, BROW)
-                        def _(m):
-                            @pl.when(((meet[p] >> m) & 1) != 0)
-                            def _():
-                                load(p, a, m, b, t)
+            slot_s[count_s[1]] = t
+            count_s[1] = count_s[1] + 1
+            total[t] = jnp.zeros_like(total[t])
+            for p in range(2):
+                def each(bits):
+                    lowest = bits & -bits
+                    load(p, bit_s[((lowest * LOWEST) & 0xFFFF) >> 12], t)
+                    return bits ^ lowest
+
+                lax.while_loop(lambda bits: bits != 0, each, meet[p])
 
     n, slots = count_s[0], count_s[1]
     for u in range(GROUP):
@@ -669,22 +671,19 @@
         pltpu.make_async_copy(done.at[0], out.at[0], store_sem).wait()
 
 
-def multiply(rows, cols, metas, blocks, right, left, partial):
-    scalars = pl.BlockSpec(memory_space=pltpu.SMEM)
+def multiply(plan, blocks, right, left):
     any_space = pl.BlockSpec(memory_space=pl.ANY)
     room = MEETINGS + GROUP
     return pl.pallas_call(
-        functools.partial(multiply_kernel, partial),
+        multiply_kernel,
         name="multiply",
         out_shape=jax.ShapeDtypeStruct((SLOTS, BS, BS), jnp.bfloat16),
-        in_specs=[scalars, scalars, scalars, any_space, any_space, any_space],
+        in_specs=[pl.BlockSpec(memory_space=pltpu.SMEM), any_space, any_space, any_space],
         out_specs=any_space,
         scratch_shapes=[
-            pltpu.SMEM((32,), jnp.int32),
-            pltpu.SMEM((64,), jnp.int32),
-            pltpu.SMEM((16,), jnp.int32),
             pltpu.SMEM((512,), jnp.int32),
             pltpu.SMEM((1024,), jnp.int32),
+            pltpu.SMEM((16,), jnp.int32),
             pltpu.SMEM((room,), jnp.int32),
             pltpu.SMEM((SLOTS,), jnp.int32),
             pltpu.SMEM((2,), jnp.int32),
@@ -698,12 +697,12 @@
             pltpu.SemaphoreType.DMA,
         ],
         compiler_params=pltpu.CompilerParams(vmem_limit_bytes=MULTIPLY_MIB * 1024 * 1024),
-    )(rows, cols, metas, blocks, right, left)
+    )(plan, blocks, right, left)
 
 
 def product(rows, cols, blocks, partial):
-    left, right, metas, flag = gather(rows, cols, blocks, partial)
-    return multiply(rows, cols, metas, blocks, right, left, partial), flag
+    left, right, plan, flag = gather(rows, cols, blocks, partial)
+    return multiply(plan, blocks, right, left), flag
 
 
 def shards(blocks, block_rows, block_cols):

time: 69.9 us -> 66.1 us (0.946)
  the two profiles are of different devices: /device:TPU:29 before, /device:TPU:1 now
where the time goes in v3:
time: 66.1 us; the launch traced here: 65.8 us
  Pallas kernels  65.1 us (98%)
  between operations  0.68 us (1%)
    pallas_call x1, Pallas kernels, gather(): pl.pallas_call(functools.partial(gather_kernel, partial), name='gather_ne...  60 us
    pallas_call x1, Pallas kernels, multiply(): pl.pallas_call(multiply_kernel, name='multiply', out_shape=jax.ShapeDtype...  5.08 us

profile of v3, /device:TPU:1, one launch (start us, length us, event | category | flops | bytes accessed | tf_op | source)
XLA Modules:
  0.0 65.8 jit_solution(14626776009602376425)
XLA Ops:
  0.0 0.0 copy-start.2
  0.0 0.0 copy-start.1
  0.0 0.0 copy-start
  0.0 60.0 %gather_needed.1 = (bf16[2,4,640,128]{3,2,1,0:T(8,128)(2,1)}, bf16[16,128,128]{2,1,0:T(8,128)(2,1)}, s32[16,128]{1,0:T(8,128)}, s32[1,1]{1,0:T(1,128)}) custom-call(s32[40]{0:T(128)} %bitcast.11, s32[40]{0:T(128)} %bitcast.13, bf16[40,128,128]{2,1,0:T(8,128)(2,1)} %bitcast.6), custom_call_target="tpu_custom_call" | custom-call | tf_op jit(solution)/shard_map/gather_needed/pallas_call | solution.py:533
  60.6 0.0 copy-done.2
  60.6 0.0 copy-done.1
  60.7 0.0 copy-done
  60.7 5.1 %multiply.3 = bf16[40,128,128]{2,1,0:T(8,128)(2,1)} custom-call(s32[16,128]{1,0:T(8,128)} %get-tuple-element.28.plan, bf16[40,128,128]{2,1,0:T(8,128)(2,1)S(1)} %bitcast.7, bf16[16,128,128]{2,1,0:T(8,128)(2,1)} %get-tuple-element.29.right, bf16[2,4,640,128]{3,2,1,0:T(8,128)(2,1)} %get-tuple-element.30.left), custom_call_target="tpu_custom_call" | custom-call | tf_op jit(solution)/shard_map/multiply/pallas_call | solution.py:677
  (1 shorter events, 0.0 us)
Async XLA Ops:
  0.0 60.6 %copy-start.2 = (s32[1,1,40]{2,1,0:T(1,128)S(1)}, s32[1,1,40]{2,1,0:T(1,128)}, u32[]{:S(2)}) copy-start(s32[1,1,40]{2,1,0:T(1,128)} %param.7) | copy-start | bytes 484
  0.0 60.6 %copy-start.1 = (s32[1,1,40]{2,1,0:T(1,128)S(1)}, s32[1,1,40]{2,1,0:T(1,128)}, u32[]{:S(2)}) copy-start(s32[1,1,40]{2,1,0:T(1,128)} %param.6) | copy-start | bytes 484
  0.0 60.7 %copy-start = (bf16[1,1,40,128,128]{4,3,2,1,0:T(8,128)(2,1)S(1)}, bf16[1,1,40,128,128]{4,3,2,1,0:T(8,128)(2,1)}, u32[]{:S(2)}) copy-start(bf16[1,1,40,128,128]{4,3,2,1,0:T(8,128)(2,1)} %param.5) | copy-start | bytes 3932164

commit v4 on v3

--- a/solution.py
+++ b/solution.py
@@ -189,15 +189,15 @@
                 do(direct(i, h))
 
         for h in ORDER:
+            @pl.when(second_root)
+            def _():
+                for i in range(PIECES):
+                    both(1, i, h, second_copy, own_second)
+
             @pl.when(first_root)
             def _():
                 for i in range(PIECES):
                     both(0, i, h, first_copy, own_first)
-
-            @pl.when(second_root)
-            def _():
-                for i in range(PIECES):
-                    both(1, i, h, second_copy, own_second)
 
     def keep(condition, source, target, do):
         @pl.when(condition)

time: 66.1 us -> 64.4 us (0.974)
  the two profiles are of different devices: /device:TPU:1 before, /device:TPU:81 now
where the time goes in v4:
time: 64.4 us; the launch traced here: 64 us
  Pallas kernels  63.3 us (98%)
  between operations  0.68 us (1%)
    pallas_call x1, Pallas kernels, gather(): pl.pallas_call(functools.partial(gather_kernel, partial), name='gather_ne...  58.4 us
    pallas_call x1, Pallas kernels, multiply(): pl.pallas_call(multiply_kernel, name='multiply', out_shape=jax.ShapeDtype...  4.92 us

profile of v4, /device:TPU:81, one launch (start us, length us, event | category | flops | bytes accessed | tf_op | source)
XLA Modules:
  0.0 64.0 jit_solution(9181579111481781675)
XLA Ops:
  0.0 0.0 copy-start.2
  0.0 0.0 copy-start.1
  0.0 0.0 copy-start
  0.0 58.4 %gather_needed.1 = (bf16[2,4,640,128]{3,2,1,0:T(8,128)(2,1)}, bf16[16,128,128]{2,1,0:T(8,128)(2,1)}, s32[16,128]{1,0:T(8,128)}, s32[1,1]{1,0:T(1,128)}) custom-call(s32[40]{0:T(128)} %bitcast.11, s32[40]{0:T(128)} %bitcast.13, bf16[40,128,128]{2,1,0:T(8,128)(2,1)} %bitcast.6), custom_call_target="tpu_custom_call" | custom-call | tf_op jit(solution)/shard_map/gather_needed/pallas_call | solution.py:533
  59.1 0.0 copy-done.2
  59.1 0.0 copy-done.1
  59.1 0.0 copy-done
  59.1 4.9 %multiply.3 = bf16[40,128,128]{2,1,0:T(8,128)(2,1)} custom-call(s32[16,128]{1,0:T(8,128)} %get-tuple-element.28.plan, bf16[40,128,128]{2,1,0:T(8,128)(2,1)S(1)} %bitcast.7, bf16[16,128,128]{2,1,0:T(8,128)(2,1)} %get-tuple-element.29.right, bf16[2,4,640,128]{3,2,1,0:T(8,128)(2,1)} %get-tuple-element.30.left), custom_call_target="tpu_custom_call" | custom-call | tf_op jit(solution)/shard_map/multiply/pallas_call | solution.py:677
  (1 shorter events, 0.0 us)
Async XLA Ops:
  0.0 59.1 %copy-start.2 = (s32[1,1,40]{2,1,0:T(1,128)S(1)}, s32[1,1,40]{2,1,0:T(1,128)}, u32[]{:S(2)}) copy-start(s32[1,1,40]{2,1,0:T(1,128)} %param.7) | copy-start | bytes 484
  0.0 59.1 %copy-start.1 = (s32[1,1,40]{2,1,0:T(1,128)S(1)}, s32[1,1,40]{2,1,0:T(1,128)}, u32[]{:S(2)}) copy-start(s32[1,1,40]{2,1,0:T(1,128)} %param.6) | copy-start | bytes 484
  0.0 59.1 %copy-start = (bf16[1,1,40,128,128]{4,3,2,1,0:T(8,128)(2,1)S(1)}, bf16[1,1,40,128,128]{4,3,2,1,0:T(8,128)(2,1)}, u32[]{:S(2)}) copy-start(bf16[1,1,40,128,128]{4,3,2,1,0:T(8,128)(2,1)} %param.5) | copy-start | bytes 3932164

commit v5 on v4

--- a/solution.py
+++ b/solution.py
@@ -30,7 +30,7 @@
     partial,
     rows_s, cols_s, blocks,
     left, right, plan, flag,
-    metas, held, stage, packed, meta, below_meta, root_meta, order_v, order_s, need_v, need_s, onward, aside,
+    plan_v, metas, held, stage, packed, meta, below_meta, root_meta, order_v, order_s, need_v, need_s, onward, aside,
     chip_flags, z_flags, y_flags, flag_v,
     local_sem, root_sem, piece_sem, onward_sem, aside_sem, cross_sem, near_sem, x_sem, core_sem,
     shift_send, shift_recv, meta_send, meta_recv, flag_send, flag_recv,
@@ -49,6 +49,7 @@
 
     across = mirrored(r)
     across_below = (across + N_ROW - 1) % N_ROW
+    aside_to, aside_of = mirrored(below), (across + 1) % N_ROW
     first_root = c == r // 2
     second_root = c == below // 2
     first_panel, second_panel = k == 0, k == 1
@@ -57,7 +58,7 @@
     near = zh == home(r)
     far = jnp.logical_not(near)
     near_first = jnp.logical_and(first_panel, near)
-    aside_first = jnp.logical_and(first_panel, far)
+    aside_first = jnp.logical_and(first_panel, zh == home(aside_of))
     near_second = jnp.logical_and(second_panel, zh == home(below))
     aside_second = jnp.logical_and(second_panel, zh == home(across_below))
 
@@ -81,7 +82,7 @@
             greet(row, col)
 
     greet_if(jnp.logical_and(first_panel, far), r, other)
-    greet_if(jnp.logical_and(first_panel, far), across, other)
+    greet_if(jnp.logical_and(first_panel, far), aside_to, other)
     greet_if(jnp.logical_and(second_panel, far), above, other)
     greet_if(jnp.logical_and(second_panel, far), mirrored(above), other)
     greet(above, r // 2)
@@ -89,7 +90,7 @@
     greet_if(jnp.logical_and(second_panel, near), above, same)
     greet(above, c)
     greet_if(jnp.logical_and(near_first, jnp.logical_not(own_first)), r, r // 2)
-    greet_if(aside_first, across, across // 2)
+    greet_if(aside_first, aside_of, aside_of // 2)
     greet_if(jnp.logical_and(near_second, jnp.logical_not(own_second)), r, below // 2)
     greet_if(aside_second, across, across_below // 2)
     if partial:
@@ -176,7 +177,8 @@
 
     def aside_copy(role, i, h):
         return remote(
-            chunk(stage.at[role, i], h), chunk(aside, h), root_sem.at[role, 1, i, h], aside_sem.at[h], across, at(i, role)
+            chunk(stage.at[role, i], h), chunk(aside, h), root_sem.at[role, 1, i, h], aside_sem.at[h],
+            across if role else aside_to, at(i, role),
         )
 
     def for_root_copies(do):
@@ -245,7 +247,7 @@
         return pass_on(1, x, h, near_sem.at[h], below, same, chunk(onward, h))
 
     def from_aside(role, h):
-        return pass_on(role, x, h, cross_sem.at[h], across if role == 0 else across_below, other, chunk(aside, h))
+        return pass_on(role, x, h, cross_sem.at[h], aside_of if role == 0 else across_below, other, chunk(aside, h))
 
     def x_copy(n, h):
         return pass_on(k, x, h, x_sem.at[n, h], r, at(ring[n], k))
@@ -318,7 +320,6 @@
 
             if h in STRAIGHT:
                 straight_first(h).start()
-            spread(h)
 
     @pl.when(aside_first)
     def _():
@@ -335,6 +336,7 @@
 
             if h in STRAIGHT:
                 straight_second(h).start()
+        for h in ORDER:
             to_near(h).start()
 
     @pl.when(aside_second)
@@ -405,21 +407,22 @@
         needs.wait()
         for s in range(ROOM):
             packed[s] = held[jnp.clip(need_s[s, 0], 0, SLOTS - 1)]
-        for i in range(parts):
-            shift_copy(i).start()
+        shift_copy(0).start()
         send_flags(chip_peers, chip_flags, x * 2 + k, 0)
 
     if partial:
         flag_v[1] = join_flags(chip_flags, 8, 0)
         send_flags(z_peers, z_flags, z, 1)
 
-    @pl.when(jnp.logical_not(near_first))
-    def _():
-        for h in ORDER:
+    for h in ORDER:
+        @pl.when(jnp.logical_not(near_first))
+        def _():
             arrived(k, x, h)
-            spread(h)
-
-    if partial:
+
+        spread(h)
+
+    if partial:
+        shift_copy(1).start()
         flag_v[2] = join_flags(z_flags, 16, 1)
         send_flags(y_peers, y_flags, y, 2)
 
@@ -460,7 +463,9 @@
     table = jnp.zeros((16, 128), jnp.int32)
     for i, entry in enumerate(entries):
         table = jnp.where(sub16 == i, entry, table)
-    plan[...] = table
+    plan_v[...] = table
+    plan_out = pltpu.make_async_copy(plan_v, plan, local_sem.at[1])
+    plan_out.start()
 
     for h in ORDER:
         for i in range(PIECES):
@@ -474,6 +479,7 @@
     else:
         flag[0, 0] = 0
 
+    plan_out.wait()
     for_root_copies(lambda copy: copy.wait_send())
 
     @pl.when(first_root)
@@ -540,8 +546,9 @@
             jax.ShapeDtypeStruct((1, 1), jnp.int32),
         ),
         in_specs=[scalars, scalars, any_space],
-        out_specs=(any_space, any_space, pl.BlockSpec(memory_space=pltpu.VMEM), scalars),
+        out_specs=(any_space, any_space, any_space, scalars),
         scratch_shapes=[
+            pltpu.VMEM((16, 128), jnp.int32),
             pltpu.VMEM((3, *tile), jnp.int32),
             pltpu.VMEM((SLOTS, BS, BS), jnp.bfloat16),
             pltpu.VMEM((2, PIECES, PIECE_ROWS, BS), jnp.bfloat16),

time: 64.4 us -> 62.8 us (0.975)
  the two profiles are of different devices: /device:TPU:81 before, /device:TPU:1 now
where the time goes in v5:
time: 62.8 us; the launch traced here: 62.7 us
  Pallas kernels  62 us (99%)
  between operations  0.68 us (1%)
    pallas_call x1, Pallas kernels, gather(): pl.pallas_call(functools.partial(gather_kernel, partial), name='gather_ne...  55.9 us
    pallas_call x1, Pallas kernels, multiply(): pl.pallas_call(multiply_kernel, name='multiply', out_shape=jax.ShapeDtype...  6.11 us

profile of v5, /device:TPU:1, one launch (start us, length us, event | category | flops | bytes accessed | tf_op | source)
XLA Modules:
  0.0 62.7 jit_solution(1217303392382891227)
XLA Ops:
  0.0 0.0 copy-start.2
  0.0 0.0 copy-start.1
  0.0 0.0 copy-start
  0.0 55.9 %gather_needed.1 = (bf16[2,4,640,128]{3,2,1,0:T(8,128)(2,1)}, bf16[16,128,128]{2,1,0:T(8,128)(2,1)}, s32[16,128]{1,0:T(8,128)}, s32[1,1]{1,0:T(1,128)}) custom-call(s32[40]{0:T(128)} %bitcast.11, s32[40]{0:T(128)} %bitcast.13, bf16[40,128,128]{2,1,0:T(8,128)(2,1)} %bitcast.6), custom_call_target="tpu_custom_call" | custom-call | tf_op jit(solution)/shard_map/gather_needed/pallas_call | solution.py:539
  56.6 0.0 copy-done.2
  56.6 0.0 copy-done.1
  56.6 0.0 copy-done
  56.6 6.1 %multiply.3 = bf16[40,128,128]{2,1,0:T(8,128)(2,1)} custom-call(s32[16,128]{1,0:T(8,128)} %get-tuple-element.28.plan, bf16[40,128,128]{2,1,0:T(8,128)(2,1)S(1)} %bitcast.7, bf16[16,128,128]{2,1,0:T(8,128)(2,1)} %get-tuple-element.29.right, bf16[2,4,640,128]{3,2,1,0:T(8,128)(2,1)} %get-tuple-element.30.left), custom_call_target="tpu_custom_call" | custom-call | tf_op jit(solution)/shard_map/multiply/pallas_call | solution.py:684
  (1 shorter events, 0.0 us)
Async XLA Ops:
  0.0 56.6 %copy-start.2 = (s32[1,1,40]{2,1,0:T(1,128)S(1)}, s32[1,1,40]{2,1,0:T(1,128)}, u32[]{:S(2)}) copy-start(s32[1,1,40]{2,1,0:T(1,128)} %param.7) | copy-start | bytes 484
  0.0 56.6 %copy-start.1 = (s32[1,1,40]{2,1,0:T(1,128)S(1)}, s32[1,1,40]{2,1,0:T(1,128)}, u32[]{:S(2)}) copy-start(s32[1,1,40]{2,1,0:T(1,128)} %param.6) | copy-start | bytes 484
  0.0 56.6 %copy-start = (bf16[1,1,40,128,128]{4,3,2,1,0:T(8,128)(2,1)S(1)}, bf16[1,1,40,128,128]{4,3,2,1,0:T(8,128)(2,1)}, u32[]{:S(2)}) copy-start(bf16[1,1,40,128,128]{4,3,2,1,0:T(8,128)(2,1)} %param.5) | copy-start | bytes 3932164
